TPU v7x, 512 devices: a whole 4x8x8 slice. The times are simulated.
512 devices in a mesh: tile: 128 (over y, z, core), dp: 4 (over x).
Axes of the slice: x: 4, y: 8, z: 8, core: 2. Of those that a mesh axis runs over, the one named last changes fastest.
Arguments:
- features: bfloat16 [4, 1024, 128, 128], P('dp', 'tile'), may hold values from -6 to 6
- w_sub: bfloat16 [27, 128, 128], replicated, may hold values from -0.109375 to 0.109375
- w_down: bfloat16 [8, 128, 256], replicated, may hold values from -0.1875 to 0.1875
- cotangent: bfloat16 [4, 512, 128, 256], P('dp', 'tile'), may hold values from -6 to 6
- vox_mask: int32 [4, 1024, 128], P('dp', 'tile'), may hold values from 0 to 1, as said below
- nbr_owner: int32 [4, 1024, 27], P('dp', 'tile'), may hold values from -1 to 127, as said below
- nbr_slot: int32 [4, 1024, 27], P('dp', 'tile'), may hold values from 0 to 7, as said below
- voxel_map: int32 [4, 1024, 27, 128], P('dp', 'tile'), may hold values from -1 to 127, as said below
- parent_slot: int32 [4, 1024], P('dp', 'tile'), may hold values from 0 to 3, as said below
- parent_octant: int32 [4, 1024], P('dp', 'tile'), may hold values from 0 to 7, as said below
Outputs:
- coarse_out: bfloat16 [4, 512, 128, 256], P('dp', 'tile')
- grad_input: bfloat16 [4, 1024, 128, 128], P('dp', 'tile')
- grad_sub_flat: float32 [442368], P('tile')
- grad_down_flat: float32 [262144], P('tile')
Inputs may be any that keep to these rules, and one draw needn't show every extreme that they name: `vox_mask`: in each tile the slots that hold only zeros lie just before its last 2 slots. `nbr_owner`: A neighbour lies on the block's own tile, on the tile before it (then in one of that tile's last 2 slots, and only for the first 2 blocks of a tile) or on the tile after it (then in one of its first 2 slots, and only for the last 2 blocks of a tile). Offset 13 is the block itself. `nbr_slot`: 0 where there is no neighbour. `voxel_map`: at offset 13 every voxel reads itself. `parent_slot`: each coarse block of a tile receives exactly two fine blocks of that tile. `parent_octant`: the two fine blocks of one coarse block have different octants.
All inputs are finite; a program needn't handle non-finite values.
Results may differ from a plain program's by a relative error of at most 0.007.
Values may be sent and summed in bfloat16 or wider, within the bound.
A program may use at most 64 MiB of HBM per device.

v0:
```python
import functools

import jax
import jax.numpy as jnp
from jax import lax
from jax.experimental import pallas as pl
from jax.experimental.pallas import tpu as pltpu
from jax.sharding import PartitionSpec as P

FACE = 2
MESH = pl.DeviceIdType.MESH


def with_halo(x, sides, width):
    for axis, dim in sides:
        size, length = (lax.axis_size(axis), x.shape[dim])
        up = [(i, (i + 1) % size) for i in range(size - 1)]
        down = [(j, i) for i, j in up]
        last = lax.slice_in_dim(x, length - width, length, axis=dim)
        first = lax.slice_in_dim(x, 0, width, axis=dim)
        before = lax.ppermute(last, axis, up)
        after = lax.ppermute(first, axis, down)
        x = jnp.concatenate([before, x, after], axis=dim)
    return x


TILE_ROWS = 8
SUB_T, DOWN_T = 7, 4
CHUNK_T = 6


def child_order(shape):
    new = lax.broadcasted_iota(jnp.int32, shape, 1)
    child, place = new // 16, new % 16
    z = 2 * (place // 4) + child // 4
    y = 2 * ((place // 2) % 2) + (child // 2) % 2
    x = 2 * (place % 2) + child % 2
    return 16 * z + 4 * y + x


def local_kernel(
    sizes, pos_ref, ext_ref, map_ref, ws_ref, wd_ref, cot_ref, mask_ref, tgt_ref,
    coarse_ref, acc_ref, parts_ref,
    picks, gathered, ext_t, ws_t, map_p, pre_t, hidden, factor, dpre, pairs, grad_sub, grad_down,
):
    f32, bf16 = jnp.float32, jnp.bfloat16
    offsets, voxels, wide = picks.shape
    blocks = wide // voxels
    channels = ws_ref.shape[1]

    def dot(a, b, dims=((1,), (0,))):
        return lax.dot_general(a, b, (dims, ((), ())), preferred_element_type=f32)

    lanes = lambda b: pl.ds(b * voxels, voxels)
    perm = (
        lax.broadcasted_iota(jnp.int32, (voxels, voxels), 0) == child_order((voxels, voxels))
    ).astype(bf16)
    for e in range(ext_ref.shape[0]):
        ext_t[e] = ext_ref[e].T
    map_p[...] = dot(map_ref[...].astype(bf16), perm)
    keep = dot(mask_ref[...].astype(bf16), perm)
    row_ids = lax.broadcasted_iota(jnp.int32, (voxels, voxels), 0).astype(f32)

    def forward(k, c):
        ws_t[:, pl.ds(pl.multiple_of(k * channels, channels), channels)] = ws_ref[k].T
        rows = map_p[pl.ds(pl.multiple_of(k * blocks, blocks), blocks), :]
        for b in range(blocks):
            e = pos_ref[b, k]
            row = rows[b:b + 1] - jnp.where(e < 0, 1000.0, 0.0)
            tile = (row_ids == row).astype(bf16)
            picks[k, :, lanes(b)] = tile
            gathered[k, :, lanes(b)] = dot(ext_t[jnp.maximum(e, 0)], tile).astype(bf16)
        return c

    lax.fori_loop(0, offsets, forward, 0)

    flat = gathered.reshape(offsets * voxels, wide)
    for p in range(blocks // 2):
        cols = pl.ds(p * 2 * voxels, 2 * voxels)
        pre_t[:, cols] = dot(ws_t[...], flat[:, cols])
    for b in range(blocks):
        pre = pre_t[:, lanes(b)]
        sig = jax.nn.sigmoid(pre)
        keep_b = keep[b:b + 1]
        hid = (keep_b * (pre * sig)).T.astype(bf16)
        for c in range(8):
            hidden[b * 16:(b + 1) * 16, c * channels:(c + 1) * channels] = hid[c * 16:(c + 1) * 16]
        factor[lanes(b), :] = (keep_b * sig * (1.0 + pre * (1.0 - sig))).T
    scatter = (
        lax.broadcasted_iota(jnp.int32, (cot_ref.shape[0], tgt_ref.shape[1]), 0) == tgt_ref[...]
    ).astype(bf16)
    partial_value = dot(hidden[...], wd_ref[...]).astype(bf16)
    coarse_ref[...] = dot(scatter, partial_value).astype(bf16)
    picked = dot(scatter, cot_ref[...], ((0,), (0,))).astype(bf16)
    dchildren = dot(picked, wd_ref[...], ((1,), (1,)))
    grad_down[...] = dot(hidden[...], picked, ((0,), (0,)))
    pairs[...] = jnp.zeros_like(pairs)
    for b in range(blocks):
        for c in range(8):
            rows = slice(b * voxels + c * 16, b * voxels + (c + 1) * 16)
            part = dchildren[b * 16:(b + 1) * 16, c * channels:(c + 1) * channels]
            dpre[rows, :] = (part * factor[rows, :]).astype(bf16)
        half = (b % 2) * voxels
        pairs[b // 2, half:half + voxels, half:half + voxels] = dpre[lanes(b), :]

    acc_ref[...] = jnp.zeros_like(acc_ref)

    def backward(k, c):
        at = pl.ds(pl.multiple_of(k * channels, channels), channels)
        grad_sub[at, :] = dot(gathered[k], dpre[...])
        weight = ws_ref[k]
        for p in range(blocks // 2):
            spread = dot(picks[k, :, pl.ds(p * 2 * voxels, 2 * voxels)], pairs[p]).astype(bf16)
            for i in range(2):
                e = jnp.maximum(pos_ref[2 * p + i, k], 0)
                term = dot(spread[:, i * channels:(i + 1) * channels], weight, ((1,), (1,)))
                acc_ref[e] += term
        return c

    lax.fori_loop(0, offsets, backward, 0)

    nx, ny, nz = sizes
    grad_sub[offsets * channels:, :] = jnp.zeros((TILE_ROWS, channels), f32)
    chip_rows = offsets * channels // (ny * nz)
    for y in range(ny):
        for z in range(nz):
            for i in range(SUB_T + DOWN_T):
                order = z * (SUB_T + DOWN_T) + i
                w, p = order % (2 * nx), order // (2 * nx)
                if i < SUB_T:
                    start = (y * nz + z) * chip_rows + i * TILE_ROWS
                    tile = grad_sub[start:start + TILE_ROWS, :]
                else:
                    m = i - SUB_T
                    start = y * 128 + z * 16 + (m % 2) * TILE_ROWS
                    tile = grad_down[start:start + TILE_ROWS, (m // 2) * 128:(m // 2 + 1) * 128]
                row = (p % CHUNK_T) * TILE_ROWS
                parts_ref[w // nx, p // CHUNK_T, w % nx, y, row:row + TILE_ROWS, :] = tile
    for w in range(2 * nx):
        row = (CHUNK_T - 1) * TILE_ROWS
        for y in range(ny):
            parts_ref[w // nx, G - 1, w % nx, y, row:row + TILE_ROWS, :] = jnp.zeros(
                (TILE_ROWS, 128), f32
            )


def local_pass(pos, ext, voxel_map, w_sub, w_down, cot, mask, tgt, sizes):
    nx, ny, nz = sizes
    offsets, channels, _ = w_sub.shape
    blocks, voxels = mask.shape
    f32, bf16 = jnp.float32, jnp.bfloat16
    wide = blocks * voxels
    vmem = pl.BlockSpec(memory_space=pltpu.VMEM)
    return pl.pallas_call(
        functools.partial(local_kernel, sizes),
        out_shape=(
            jax.ShapeDtypeStruct((cot.shape[0], cot.shape[1]), bf16),
            jax.ShapeDtypeStruct(ext.shape, f32),
            jax.ShapeDtypeStruct((2, G, nx, ny, CHUNK_T * TILE_ROWS, 128), f32),
        ),
        in_specs=[pl.BlockSpec(memory_space=pltpu.SMEM)] + [vmem] * 7,
        out_specs=(vmem,) * 3,
        scratch_shapes=[
            pltpu.VMEM((offsets, voxels, wide), bf16),
            pltpu.VMEM((offsets, channels, wide), bf16),
            pltpu.VMEM((ext.shape[0], channels, voxels), bf16),
            pltpu.VMEM((channels, offsets * channels), bf16),
            pltpu.VMEM((offsets * blocks, voxels), f32),
            pltpu.VMEM((channels, wide), f32),
            pltpu.VMEM((wide // 8, 8 * channels), bf16),
            pltpu.VMEM((wide, channels), f32),
            pltpu.VMEM((wide, channels), bf16),
            pltpu.VMEM((blocks // 2, 2 * voxels, 2 * channels), bf16),
            pltpu.VMEM((offsets * channels + TILE_ROWS, channels), f32),
            pltpu.VMEM((8 * channels, cot.shape[1]), f32),
        ],
        compiler_params=pltpu.CompilerParams(vmem_limit_bytes=56 * 1024 * 1024),
    )(pos, ext, voxel_map, w_sub, w_down, cot, mask, tgt)


G = 2
SLOT = 16


def reduce_kernel(
    sizes, scale, parts_ref, sub_ref, down_ref, send0, recv0, acc1, send1, recv1, acc2, send2, recv2,
    tiles, recv3, fin, gath, share, ss0, rs0, ss1, rs1, ss2, rs2, ss3, rs3, ss4, rs4,
):
    nx, ny, nz = sizes
    workers = 2 * nx
    per_chip = SUB_T + DOWN_T
    tile = lax.axis_index("tile")
    x = lax.axis_index("dp")
    core = lax.rem(tile, 2)
    z = lax.rem(tile // 2, nz)
    y = tile // (2 * nz)
    other = 1 - core
    f32, bf16 = jnp.float32, jnp.bfloat16

    def place(yy, zz, cc):
        return (yy * nz + zz) * 2 + cc

    x_peers = [lax.rem(x + d, nx) for d in range(1, nx)]
    y_peers = [lax.rem(y + d, ny) for d in range(1, ny)]
    z_peers = [lax.rem(z + d, nz) for d in range(1, nz)]
    group = [(f, d) for f in (0, 1) for d in range(nx) if (f, d) != (0, 0)]

    def worker(f, d):
        cc = core if f == 0 else other
        return cc, lax.rem(x + d, nx)

    barrier = pltpu.get_barrier_semaphore()
    for f, d in group:
        cc, xx = worker(f, d)
        pl.semaphore_signal(barrier, inc=1, device_id=(place(y, z, cc), xx), device_id_type=MESH)
    for yy in y_peers:
        pl.semaphore_signal(barrier, inc=1, device_id=(place(yy, z, core), x), device_id_type=MESH)
    for zz in z_peers:
        pl.semaphore_signal(barrier, inc=1, device_id=(place(y, zz, core), x), device_id_type=MESH)

    copies = []

    def send(src, dst, ss, rs, t, xx):
        copy = pltpu.make_async_remote_copy(
            src_ref=src, dst_ref=dst, send_sem=ss, recv_sem=rs,
            device_id=(t, xx), device_id_type=MESH,
        )
        copy.start()
        copies.append(copy)
        return copy

    def cast_half(g):
        def body(i, c):
            send0[g, i] = parts_ref[other, g, i].astype(bf16)
            return c
        lax.fori_loop(0, nx, body, 0)

    cast_half(0)
    pl.semaphore_wait(barrier, len(group) + ny - 1 + nz - 1)
    step0 = []
    for g in range(G):
        if g:
            cast_half(g)
        step0.append(send(send0.at[g], recv0.at[g], ss0.at[g], rs0.at[g], place(y, z, other), x))

    step1 = []
    for g in range(G):
        step0[g].wait_recv()

        def body(i, c):
            total = parts_ref[core, g, i] + recv0[g, i].astype(f32)
            acc1[g, i] = total
            send1[g, i] = total.astype(bf16)
            return c

        lax.fori_loop(0, nx, body, 0)
        step1.append([
            send(send1.at[g, xx], recv1.at[d, g], ss1.at[d, g], rs1.at[d, g], tile, xx)
            for d, xx in enumerate(x_peers)
        ])

    step2 = []
    for g in range(G):
        for copy in step1[g]:
            copy.wait_recv()

        def body(i, c):
            total = acc1[g, x, i]
            for d in range(nx - 1):
                total = total + recv1[d, g, i].astype(f32)
            acc2[g, i] = total
            send2[g, i] = total.astype(bf16)
            return c

        lax.fori_loop(0, ny, body, 0)
        step2.append([
            send(send2.at[g, yy], recv2.at[d, g], ss2.at[d, g], rs2.at[d, g], place(yy, z, core), x)
            for d, yy in enumerate(y_peers)
        ])

    for g in range(G):
        for copy in step2[g]:
            copy.wait_recv()
        total = acc2[g, y]
        for d in range(ny - 1):
            total = total + recv2[d, g].astype(f32)
        for j in range(CHUNK_T):
            tiles[g * CHUNK_T + j] = total[j * TILE_ROWS:(j + 1) * TILE_ROWS]
    tiles[G * CHUNK_T] = jnp.zeros((TILE_ROWS, 128), f32)

    mine = core * nx + x

    def first_tile(zz):
        begin = zz * per_chip
        return (begin + lax.rem(mine + per_chip * workers * nz - begin, workers)) // workers

    step3 = [
        send(
            tiles.at[pl.ds(first_tile(zz), 2)], recv3.at[d], ss3.at[d], rs3.at[d],
            place(y, zz, core), x,
        )
        for d, zz in enumerate(z_peers)
    ]
    own = first_tile(z)
    for copy in step3:
        copy.wait_recv()
    for j in range(2):
        total = tiles[own + j]
        for d in range(nz - 1):
            total = total + recv3[d, j]
        fin[j] = total * scale
    step4 = []
    for i, (f, d) in enumerate(group):
        cc, xx = worker(f, d)
        step4.append(send(fin, gath.at[mine], ss4.at[i], rs4.at[i], place(y, z, cc), xx))
    gath[mine] = fin[...]
    for copy in step4:
        copy.wait_recv()
    begin = z * per_chip
    for i in range(SUB_T):
        share[i * TILE_ROWS:(i + 1) * TILE_ROWS, :] = gath[lax.rem(begin + i, workers), i // workers]
    rows = sub_ref.shape[0]
    low, high = share[0:rows, :], share[rows:2 * rows, :]
    pick = (core == 0).astype(f32)
    sub_ref[...] = low * pick + high * (1.0 - pick)
    for h in range(2):
        both = [
            gath[lax.rem(begin + SUB_T + 2 * h + j, workers), (SUB_T + 2 * h + j) // workers]
            for j in range(2)
        ]
        down_ref[:, h * 128:(h + 1) * 128] = both[0] * pick + both[1] * (1.0 - pick)
    for copy in copies:
        copy.wait_send()


def reduce_parts(parts, sizes, scale, sub_rows):
    nx, ny, nz = sizes
    rows = parts.shape[4]
    f32, bf16 = jnp.float32, jnp.bfloat16
    dma = pltpu.SemaphoreType.DMA
    lanes = parts.shape[5]
    group = 2 * nx - 1
    vmem = pl.BlockSpec(memory_space=pltpu.VMEM)
    return pl.pallas_call(
        functools.partial(reduce_kernel, sizes, scale),
        out_shape=(
            jax.ShapeDtypeStruct((sub_rows, lanes), f32),
            jax.ShapeDtypeStruct((TILE_ROWS, 2 * lanes), f32),
        ),
        in_specs=[vmem],
        out_specs=(vmem, vmem),
        scratch_shapes=[
            pltpu.VMEM((G, nx, ny, rows, lanes), bf16),
            pltpu.VMEM((G, nx, ny, rows, lanes), bf16),
            pltpu.VMEM((G, nx, ny, rows, lanes), f32),
            pltpu.VMEM((G, nx, ny, rows, lanes), bf16),
            pltpu.VMEM((nx - 1, G, ny, rows, lanes), bf16),
            pltpu.VMEM((G, ny, rows, lanes), f32),
            pltpu.VMEM((G, ny, rows, lanes), bf16),
            pltpu.VMEM((ny - 1, G, rows, lanes), bf16),
            pltpu.VMEM((G * CHUNK_T + 1, TILE_ROWS, lanes), f32),
            pltpu.VMEM((nz - 1, 2, TILE_ROWS, lanes), f32),
            pltpu.VMEM((2, TILE_ROWS, lanes), f32),
            pltpu.VMEM((2 * nx, 2, TILE_ROWS, lanes), f32),
            pltpu.VMEM((SUB_T * TILE_ROWS, lanes), f32),
            dma((G,)), dma((G,)),
            dma((nx - 1, G)), dma((nx - 1, G)),
            dma((ny - 1, G)), dma((ny - 1, G)),
            dma((nz - 1,)), dma((nz - 1,)),
            dma((group,)), dma((group,)),
        ],
        compiler_params=pltpu.CompilerParams(
            collective_id=0, has_side_effects=True, vmem_limit_bytes=48 * 1024 * 1024
        ),
    )(parts)


def on_device(
    features,
    w_sub,
    w_down,
    cotangent,
    vox_mask,
    nbr_owner,
    nbr_slot,
    voxel_map,
    parent_slot,
    parent_octant,
):
    blocks = features.shape[1]
    voxels = features.shape[2]
    channels = features.shape[3]
    coarse_count = cotangent.shape[1]
    tile_index = lax.axis_index("tile")
    active = vox_mask[0] > 0
    keep_f = active.reshape(-1, 1).astype(jnp.float32)
    masked = jnp.where(active[:, :, None], features[0], jnp.zeros((), jnp.bfloat16))
    halo_width = FACE
    extended = with_halo(masked, (("tile", 0),), halo_width)
    ext_count = extended.shape[0]
    owner_tile = nbr_owner[0]
    slot_index = nbr_slot[0]
    position = jnp.where(
        owner_tile == tile_index - 1,
        slot_index - (blocks - halo_width),
        jnp.where(
            owner_tile == tile_index, halo_width + slot_index, halo_width + blocks + slot_index
        ),
    )
    position = jnp.where(owner_tile >= 0, position, -1)
    sizes = (lax.axis_size("dp"), 8, lax.axis_size("tile") // 16)
    maps = jnp.transpose(voxel_map[0], (1, 0, 2)).reshape(-1, voxels)
    place = jnp.arange(16, dtype=jnp.int32)[None, :]
    octant = parent_octant[0][:, None]
    within = (
        16 * (4 * (octant // 4) + place // 4)
        + 4 * (2 * ((octant // 2) % 2) + (place // 2) % 2)
        + 2 * (octant % 2) + place % 2
    )
    target = (parent_slot[0][:, None] * cotangent.shape[2] + within).reshape(1, -1)
    coarse, grad_rows, parts = local_pass(
        position, extended, maps, w_sub, w_down.reshape(-1, w_down.shape[2]),
        cotangent[0].reshape(-1, cotangent.shape[3]), vox_mask[0], target, sizes,
    )
    coarse_out = coarse.reshape(cotangent.shape)
    own_grad = grad_rows[halo_width : halo_width + blocks]
    outgoing = jnp.concatenate([grad_rows[:halo_width], grad_rows[halo_width + blocks :]], axis=0)
    returned = with_halo(outgoing.astype(jnp.bfloat16), (("tile", 0),), halo_width).astype(
        outgoing.dtype
    )
    own_grad = own_grad.at[:halo_width].add(returned[:halo_width])
    own_grad = own_grad.at[blocks - halo_width :].add(returned[3 * halo_width :])
    grad_input = (keep_f.reshape(blocks, voxels, 1) * own_grad).astype(jnp.bfloat16)[None]
    grad_scale = float(lax.axis_size("dp") * lax.axis_size("tile") * blocks * voxels) ** (-0.5)
    sub_rows = w_sub.size // channels // lax.axis_size("tile")
    share_sub, share_down = reduce_parts(parts, sizes, grad_scale, sub_rows)
    return (coarse_out, grad_input, share_sub.reshape(-1), share_down.reshape(-1))


def solution(mesh):
    in_specs = (
        P("dp", "tile", None, None),
        P(),
        P(),
        P("dp", "tile", None, None),
        P("dp", "tile", None),
        P("dp", "tile", None),
        P("dp", "tile", None),
        P("dp", "tile", None, None),
        P("dp", "tile"),
        P("dp", "tile"),
    )
    out_specs = (P("dp", "tile", None, None), P("dp", "tile", None, None), P("tile"), P("tile"))
    return jax.shard_map(
        on_device, mesh=mesh, in_specs=in_specs, out_specs=out_specs, check_vma=False
    )
```

profile of v0, /device:TPU:1, one launch (start us, length us, event | category | flops | bytes accessed | tf_op | source)
XLA Modules:
  0.0 105.8 jit_solution(466619843101199379)
XLA Ops:
  0.6 0.7 fusion.8
  1.3 1.1 %bitcast_select_fusion = bf16[8,128,128]{2,1,0:T(8,128)(2,1)S(1)} fusion(bf16[1,8,128,128]{3,2,1,0:T(8,128)(2,1)} %param.14, pred[8,128]{1,0:T(8,128)(4,1)S(1)} %get-tuple-element.39), kind=kLoop, calls=%fused_computation.3 | loop fusion | flops 131072 | bytes 525312 | tf_op jit(solution)/shard_map/jit(_where)/select_n | solution.py:397
  2.5 5.4 %collective-permute-start = (bf16[2,128,128]{2,1,0:T(8,128)(2,1)S(1)}, bf16[2,128,128]{2,1,0:T(8,128)(2,1)S(1)}, u32[]{:S(2)}, u32[]{:S(2)}) collective-permute-start(bf16[2,128,128]{2,1,0:T(8,128)(2,1)S(1)} %get-tuple-element.42), channel_id=1, source_target_pairs={{0,4},{4,8},{8,12},{12,16},{16,20},{20,24},{24,28},{28,32},{32,36}... | collective-permute-start | bytes 196616 | tf_op jit(solution)/shard_map/ppermute | solution.py:21
  7.9 4.7 %collective-permute-start.1 = (bf16[2,128,128]{2,1,0:T(8,128)(2,1)S(1)}, bf16[2,128,128]{2,1,0:T(8,128)(2,1)S(1)}, u32[]{:S(2)}, u32[]{:S(2)}) collective-permute-start(bf16[2,128,128]{2,1,0:T(8,128)(2,1)S(1)} %get-tuple-element.43), channel_id=1, source_target_pairs={{4,0},{8,4},{12,8},{16,12},{20,16},{24,20},{28,24},{32,28},{36,32}... | collective-permute-start | bytes 196616 | tf_op jit(solution)/shard_map/ppermute | solution.py:22
  12.6 0.7 multiply_bitcast_fusion
  13.3 0.7 fusion.7
  14.0 1.3 %select_bitcast_fusion.pos_ref = s32[8,27]{1,0:T(8,128)} fusion(s32[1,8,27]{2,1,0:T(8,128)} %param.20, s32[1,8,27]{2,1,0:T(8,128)} %param.19, s32[]{:T(128)S(6)} %axis_index.15, s32[]{:T(128)S(6)} %sub.21), kind=kLoop, calls=%fused_computation.12 | loop fusion | flops 1944 | bytes 2600 | tf_op jit(solution)/shard_map/jit(_where)/select_n | solution.py:410
  15.3 0.1 add_add_fusion
  15.3 0.6 reshape.484.tgt_ref
  15.9 0.0 collective-permute-done
  15.9 0.0 collective-permute-done.1
  15.9 0.8 pad_maximum_fusion.ext_ref
  16.7 35.6 %shard_map.129 = (bf16[512,256]{1,0:T(8,128)(2,1)}, f32[12,128,128]{2,1,0:T(8,128)}, f32[2,2,4,8,48,128]{5,4,3,2,1,0:T(8,128)}) custom-call(s32[8,27]{1,0:T(8,128)} %select_bitcast_fusion.pos_ref, bf16[12,128,128]{2,1,0:T(8,128)(2,1)} %pad_maximum_fusion.ext_ref, s32[216,128]{1,0:T(8,128)} %bitcast.52, bf16[27,128,128]{2,1,0:T(8,128)(2,1)} %ws_ref.1, ...), custom_call_target="tpu_custom_call" | custom-call | tf_op jit(solution)/shard_map/pallas_call | solution.py:154
  52.3 1.2 %convert.6 = bf16[12,128,128]{2,1,0:T(8,128)(2,1)S(1)} convert(f32[12,128,128]{2,1,0:T(8,128)} %get-tuple-element.34) | non-fusion elementwise | flops 196608 | bytes 1179648 | tf_op jit(solution)/shard_map/convert.2
  53.5 1.9 %collective-permute-start.2 = (bf16[2,128,128]{2,1,0:T(8,128)(2,1)S(1)}, bf16[2,128,128]{2,1,0:T(8,128)(2,1)S(1)}, u32[]{:S(2)}, u32[]{:S(2)}) collective-permute-start(bf16[2,128,128]{2,1,0:T(8,128)(2,1)S(1)} %get-tuple-element.40), channel_id=1, source_target_pairs={{0,4},{4,8},{8,12},{12,16},{16,20},{20,24},{24,28},{28,32},{32,36}... | collective-permute-start | bytes 196616 | tf_op jit(solution)/shard_map/ppermute | solution.py:21
  55.5 2.4 %collective-permute-start.3 = (bf16[2,128,128]{2,1,0:T(8,128)(2,1)S(1)}, bf16[2,128,128]{2,1,0:T(8,128)(2,1)S(1)}, u32[]{:S(2)}, u32[]{:S(2)}) collective-permute-start(bf16[2,128,128]{2,1,0:T(8,128)(2,1)S(1)} %get-tuple-element.41), channel_id=1, source_target_pairs={{4,0},{8,4},{12,8},{16,12},{20,16},{24,20},{28,24},{32,28},{36,32}... | collective-permute-start | bytes 196616 | tf_op jit(solution)/shard_map/ppermute | solution.py:22
  57.9 1.1 %slice.76 = f32[8,128,128]{2,1,0:T(8,128)S(1)} slice(f32[12,128,128]{2,1,0:T(8,128)} %get-tuple-element.34), slice={[2:10], [0:128], [0:128]} | slice | bytes 1048576 | tf_op jit(solution)/shard_map/slice | solution.py:426
  59.0 1.9 %copy-done = f32[2,2,4,8,48,128]{5,4,3,2,1,0:T(8,128)S(1)} copy-done((f32[2,2,4,8,48,128]{5,4,3,2,1,0:T(8,128)S(1)}, f32[2,2,4,8,48,128]{5,4,3,2,1,0:T(8,128)}, u32[]{:S(2)}) %copy-start) | copy-done | bytes 3145752
  60.9 41.9 %shard_map.130 = (f32[27,128]{1,0:T(8,128)S(1)}, f32[8,256]{1,0:T(8,128)S(1)}) custom-call(f32[2,2,4,8,48,128]{5,4,3,2,1,0:T(8,128)S(1)} %copy-done), custom_call_target="tpu_custom_call" | custom-call | tf_op jit(solution)/shard_map/pallas_call | solution.py:344
  102.7 0.6 copy.14
  103.3 0.0 collective-permute-done.2
  103.3 0.9 fusion.2
  104.3 0.9 fusion
  105.2 0.6 copy.18
  (7 shorter events, 0.1 us)
Async XLA Ops:
  2.5 13.4 %collective-permute-start = (bf16[2,128,128]{2,1,0:T(8,128)(2,1)S(1)}, bf16[2,128,128]{2,1,0:T(8,128)(2,1)S(1)}, u32[]{:S(2)}, u32[]{:S(2)}) collective-permute-start(bf16[2,128,128]{2,1,0:T(8,128)(2,1)S(1)} %get-tuple-element.42), channel_id=1, source_target_pairs={{0,4},{4,8},{8,12},{12,16},{16,20},{20,24},{24,28},{28,32},{32,36}... | collective-permute-start | bytes 196616 | tf_op jit(solution)/shard_map/ppermute | solution.py:21
  7.9 8.0 %collective-permute-start.1 = (bf16[2,128,128]{2,1,0:T(8,128)(2,1)S(1)}, bf16[2,128,128]{2,1,0:T(8,128)(2,1)S(1)}, u32[]{:S(2)}, u32[]{:S(2)}) collective-permute-start(bf16[2,128,128]{2,1,0:T(8,128)(2,1)S(1)} %get-tuple-element.43), channel_id=1, source_target_pairs={{4,0},{8,4},{12,8},{16,12},{20,16},{24,20},{28,24},{32,28},{36,32}... | collective-permute-start | bytes 196616 | tf_op jit(solution)/shard_map/ppermute | solution.py:22
  53.5 49.8 %collective-permute-start.2 = (bf16[2,128,128]{2,1,0:T(8,128)(2,1)S(1)}, bf16[2,128,128]{2,1,0:T(8,128)(2,1)S(1)}, u32[]{:S(2)}, u32[]{:S(2)}) collective-permute-start(bf16[2,128,128]{2,1,0:T(8,128)(2,1)S(1)} %get-tuple-element.40), channel_id=1, source_target_pairs={{0,4},{4,8},{8,12},{12,16},{16,20},{20,24},{24,28},{28,32},{32,36}... | collective-permute-start | bytes 196616 | tf_op jit(solution)/shard_map/ppermute | solution.py:21
  55.5 47.9 %collective-permute-start.3 = (bf16[2,128,128]{2,1,0:T(8,128)(2,1)S(1)}, bf16[2,128,128]{2,1,0:T(8,128)(2,1)S(1)}, u32[]{:S(2)}, u32[]{:S(2)}) collective-permute-start(bf16[2,128,128]{2,1,0:T(8,128)(2,1)S(1)} %get-tuple-element.41), channel_id=1, source_target_pairs={{4,0},{8,4},{12,8},{16,12},{20,16},{24,20},{28,24},{32,28},{36,32}... | collective-permute-start | bytes 196616 | tf_op jit(solution)/shard_map/ppermute | solution.py:22
  59.0 1.9 %copy-start = (f32[2,2,4,8,48,128]{5,4,3,2,1,0:T(8,128)S(1)}, f32[2,2,4,8,48,128]{5,4,3,2,1,0:T(8,128)}, u32[]{:S(2)}) copy-start(f32[2,2,4,8,48,128]{5,4,3,2,1,0:T(8,128)} %get-tuple-element.35.parts_ref) | copy-start | bytes 9437188
where the time goes:
time: 106 us
  Pallas kernels  77.4 us (73%)
  starting transfers between devices  14.4 us (14%)
  other arithmetic  8.41 us (8%)
  local copies, waits for them, and re-layouts  4.79 us (5%)
    pallas_call x1, Pallas kernels, reduce_parts(): pl.pallas_call(functools.partial(reduce_kernel, sizes, scale), out_shape=...  41.9 us
    pallas_call x1, Pallas kernels, local_pass(): pl.pallas_call(functools.partial(local_kernel, sizes), out_shape=(jax.Sha...  35.6 us
    ppermute x2, starting transfers between devices, with_halo(): before = lax.ppermute(last, axis, up)  7.31 us
    ppermute x2, starting transfers between devices, with_halo(): after = lax.ppermute(first, axis, down)  7.09 us
    unnamed x4, local copies, waits for them, and re-layouts  3.09 us
  transfers between devices with their start and end apart: 4, of which 0 were waited for; matrix products, arithmetic and copies ran while one was open for 5% of the time, Pallas kernels for 40%

commit v1 on v0

v1 whole, which is shorter than its diff:
```python
import functools

import jax
import jax.numpy as jnp
from jax import lax
from jax.experimental import pallas as pl
from jax.experimental.pallas import tpu as pltpu
from jax.sharding import PartitionSpec as P

FACE = 2
MESH = pl.DeviceIdType.MESH


def with_halo(x, sides, width):
    for axis, dim in sides:
        size, length = (lax.axis_size(axis), x.shape[dim])
        up = [(i, (i + 1) % size) for i in range(size - 1)]
        down = [(j, i) for i, j in up]
        last = lax.slice_in_dim(x, length - width, length, axis=dim)
        first = lax.slice_in_dim(x, 0, width, axis=dim)
        before = lax.ppermute(last, axis, up)
        after = lax.ppermute(first, axis, down)
        x = jnp.concatenate([before, x, after], axis=dim)
    return x


TILE_ROWS = 8
HALF_T = 3


def child_order(shape):
    new = lax.broadcasted_iota(jnp.int32, shape, 1)
    child, place = new // 16, new % 16
    z = 2 * (place // 4) + child // 4
    y = 2 * ((place // 2) % 2) + (child // 2) % 2
    x = 2 * (place % 2) + child % 2
    return 16 * z + 4 * y + x


def local_kernel(
    sizes, pos_ref, ext_ref, map_ref, ws_ref, wd_ref, cot_ref, mask_ref, tgt_ref,
    coarse_ref, acc_ref, parts_ref,
    picks, gathered, ext_t, ws_t, map_p, pre_t, hidden, factor, dpre, pairs, grad_sub, grad_down,
):
    f32, bf16 = jnp.float32, jnp.bfloat16
    offsets, voxels, wide = picks.shape
    blocks = wide // voxels
    channels = ws_ref.shape[1]

    def dot(a, b, dims=((1,), (0,))):
        return lax.dot_general(a, b, (dims, ((), ())), preferred_element_type=f32)

    lanes = lambda b: pl.ds(b * voxels, voxels)
    perm = (
        lax.broadcasted_iota(jnp.int32, (voxels, voxels), 0) == child_order((voxels, voxels))
    ).astype(bf16)
    for e in range(ext_ref.shape[0]):
        ext_t[e] = ext_ref[e].T
    map_p[...] = dot(map_ref[...].astype(bf16), perm)
    keep = dot(mask_ref[...].astype(bf16), perm)
    row_ids = lax.broadcasted_iota(jnp.int32, (voxels, voxels), 0).astype(f32)

    def forward(k, c):
        ws_t[:, pl.ds(pl.multiple_of(k * channels, channels), channels)] = ws_ref[k].T
        rows = map_p[pl.ds(pl.multiple_of(k * blocks, blocks), blocks), :]
        for b in range(blocks):
            e = pos_ref[b, k]
            row = rows[b:b + 1] - jnp.where(e < 0, 1000.0, 0.0)
            tile = (row_ids == row).astype(bf16)
            picks[k, :, lanes(b)] = tile
            gathered[k, :, lanes(b)] = dot(ext_t[jnp.maximum(e, 0)], tile).astype(bf16)
        return c

    lax.fori_loop(0, offsets, forward, 0, unroll=3)

    flat = gathered.reshape(offsets * voxels, wide)
    for p in range(blocks // 2):
        cols = pl.ds(p * 2 * voxels, 2 * voxels)
        pre_t[:, cols] = dot(ws_t[...], flat[:, cols])
    for b in range(blocks):
        pre = pre_t[:, lanes(b)]
        sig = jax.nn.sigmoid(pre)
        keep_b = keep[b:b + 1]
        hid = (keep_b * (pre * sig)).T.astype(bf16)
        for c in range(8):
            hidden[b * 16:(b + 1) * 16, c * channels:(c + 1) * channels] = hid[c * 16:(c + 1) * 16]
        factor[lanes(b), :] = (keep_b * sig * (1.0 + pre * (1.0 - sig))).T
    scatter = (
        lax.broadcasted_iota(jnp.int32, (cot_ref.shape[0], tgt_ref.shape[1]), 0) == tgt_ref[...]
    ).astype(bf16)
    partial_value = dot(hidden[...], wd_ref[...]).astype(bf16)
    coarse_ref[...] = dot(scatter, partial_value).astype(bf16)
    picked = dot(scatter, cot_ref[...], ((0,), (0,))).astype(bf16)
    dchildren = dot(picked, wd_ref[...], ((1,), (1,)))
    grad_down[...] = dot(hidden[...], picked, ((0,), (0,)))
    pairs[...] = jnp.zeros_like(pairs)
    for b in range(blocks):
        for c in range(8):
            rows = slice(b * voxels + c * 16, b * voxels + (c + 1) * 16)
            part = dchildren[b * 16:(b + 1) * 16, c * channels:(c + 1) * channels]
            dpre[rows, :] = (part * factor[rows, :]).astype(bf16)
        half = (b % 2) * voxels
        pairs[b // 2, half:half + voxels, half:half + voxels] = dpre[lanes(b), :]

    acc_ref[...] = jnp.zeros_like(acc_ref)

    flat_picks = picks.reshape(offsets * voxels, wide)

    def backward(j, c):
        for q in range(3):
            k = j * 3 + q
            at = pl.ds(pl.multiple_of(k * channels, channels), channels)
            grad_sub[at, :] = dot(gathered[k], dpre[...])
        rows = pl.ds(pl.multiple_of(j * 3 * voxels, 128), 3 * voxels)
        for p in range(blocks // 2):
            spread = dot(flat_picks[rows, pl.ds(p * 2 * voxels, 2 * voxels)], pairs[p]).astype(bf16)
            for q in range(3):
                k = j * 3 + q
                weight = ws_t[:, pl.ds(pl.multiple_of(k * channels, channels), channels)]
                for i in range(2):
                    e = jnp.maximum(pos_ref[2 * p + i, k], 0)
                    acc_ref[e] += dot(spread[q*voxels:(q+1)*voxels, i * channels:(i + 1) * channels], weight)
        return c

    lax.fori_loop(0, offsets // 3, backward, 0)

    nx, ny, nz = sizes
    grad_sub[offsets * channels:, :] = jnp.zeros((TILE_ROWS, channels), f32)
    share = offsets * channels // (2 * ny * nz)
    for y in range(ny):
        for z in range(nz):
            for core in range(2):
                start = ((y * nz + z) * 2 + core) * share
                for i in range(HALF_T):
                    rows = slice(i * TILE_ROWS, (i + 1) * TILE_ROWS)
                    tile = grad_sub[start + i * TILE_ROWS:start + (i + 1) * TILE_ROWS, :]
                    parts_ref[core, 0, y, z, rows, :] = tile
                tile = grad_sub[start + HALF_T * TILE_ROWS:start + (HALF_T + 1) * TILE_ROWS, :]
                parts_ref[core, 1, z, y, 0:TILE_ROWS, :] = tile
                start = y * channels + (z * 2 + core) * TILE_ROWS
                for i in range(2):
                    rows = slice((i + 1) * TILE_ROWS, (i + 2) * TILE_ROWS)
                    tile = grad_down[start:start + TILE_ROWS, i * 128:(i + 1) * 128]
                    parts_ref[core, 1, z, y, rows, :] = tile


def local_pass(pos, ext, voxel_map, w_sub, w_down, cot, mask, tgt, sizes):
    nx, ny, nz = sizes
    offsets, channels, _ = w_sub.shape
    blocks, voxels = mask.shape
    f32, bf16 = jnp.float32, jnp.bfloat16
    wide = blocks * voxels
    vmem = pl.BlockSpec(memory_space=pltpu.VMEM)
    return pl.pallas_call(
        functools.partial(local_kernel, sizes),
        out_shape=(
            jax.ShapeDtypeStruct((cot.shape[0], cot.shape[1]), bf16),
            jax.ShapeDtypeStruct(ext.shape, f32),
            jax.ShapeDtypeStruct((2, 2, ny, nz, HALF_T * TILE_ROWS, 128), f32),
        ),
        in_specs=[pl.BlockSpec(memory_space=pltpu.SMEM)] + [vmem] * 7,
        out_specs=(vmem,) * 3,
        scratch_shapes=[
            pltpu.VMEM((offsets, voxels, wide), bf16),
            pltpu.VMEM((offsets, channels, wide), bf16),
            pltpu.VMEM((ext.shape[0], channels, voxels), bf16),
            pltpu.VMEM((channels, offsets * channels), bf16),
            pltpu.VMEM((offsets * blocks, voxels), f32),
            pltpu.VMEM((channels, wide), f32),
            pltpu.VMEM((wide // 8, 8 * channels), bf16),
            pltpu.VMEM((wide, channels), f32),
            pltpu.VMEM((wide, channels), bf16),
            pltpu.VMEM((blocks // 2, 2 * voxels, 2 * channels), bf16),
            pltpu.VMEM((offsets * channels + TILE_ROWS, channels), f32),
            pltpu.VMEM((8 * channels, cot.shape[1]), f32),
        ],
        compiler_params=pltpu.CompilerParams(vmem_limit_bytes=56 * 1024 * 1024),
    )(pos, ext, voxel_map, w_sub, w_down, cot, mask, tgt)


def reduce_kernel(
    sizes, scale, parts_ref, terms_ref, mask_ref, sub_ref, down_ref, grad_ref,
    send0, recv0, acc1, send1, recv1, acc2, recv2, recv3, share, out_b, out_a, in_b, in_a,
    ss0, rs0, ss1, rs1, ss2, rs2, ss3, rs3, ssh, rsh,
):
    nx, ny, nz = sizes
    tile = lax.axis_index("tile")
    x = lax.axis_index("dp")
    core = lax.rem(tile, 2)
    z = lax.rem(tile // 2, nz)
    y = tile // (2 * nz)
    other = 1 - core
    count = 2 * ny * nz
    f32, bf16 = jnp.float32, jnp.bfloat16

    def place(yy, zz, cc):
        return (yy * nz + zz) * 2 + cc

    x_peers = [lax.rem(x + d, nx) for d in range(1, nx)]
    y_peers = [lax.rem(y + d, ny) for d in range(1, ny)]
    z_peers = [lax.rem(z + d, nz) for d in range(1, nz)]
    after, before = lax.rem(tile + 1, count), lax.rem(tile + count - 1, count)

    barrier = pltpu.get_barrier_semaphore()
    peers = [(place(y, z, other), x), (after, x), (before, x)]
    peers += [(tile, xx) for xx in x_peers]
    peers += [(place(yy, z, core), x) for yy in y_peers]
    peers += [(place(y, zz, core), x) for zz in z_peers]
    for peer in peers:
        pl.semaphore_signal(barrier, inc=1, device_id=peer, device_id_type=MESH)

    copies = []

    def send(src, dst, ss, rs, t, xx):
        copy = pltpu.make_async_remote_copy(
            src_ref=src, dst_ref=dst, send_sem=ss, recv_sem=rs,
            device_id=(t, xx), device_id_type=MESH,
        )
        copy.start()
        copies.append(copy)
        return copy

    def cast_half(h):
        def body(i, c):
            send0[h, i] = parts_ref[other, h, i].astype(bf16)
            return c
        lax.fori_loop(0, ny, body, 0)

    blocks = grad_ref.shape[0]
    cast_half(0)
    pl.semaphore_wait(barrier, len(peers))
    step0 = [send(send0.at[0], recv0.at[0], ss0.at[0], rs0.at[0], place(y, z, other), x)]
    cast_half(1)
    step0.append(send(send0.at[1], recv0.at[1], ss0.at[1], rs0.at[1], place(y, z, other), x))
    out_b[...] = terms_ref[0:FACE].astype(bf16)
    out_a[...] = terms_ref[FACE + blocks:].astype(bf16)

    step1 = []
    for h in range(2):
        step0[h].wait_recv()

        def body(i, c):
            total = parts_ref[core, h, i] + recv0[h, i].astype(f32)
            acc1[h, i] = total
            send1[h, i] = total.astype(bf16)
            return c

        lax.fori_loop(0, ny, body, 0)
        for d in range(ny - 1):
            to = y_peers[d] if h == 0 else z_peers[d]
            t = place(to, z, core) if h == 0 else place(y, to, core)
            step1.append(send(send1.at[h, to], recv1.at[h, d], ss1.at[h, d], rs1.at[h, d], t, x))
    halo = [
        send(out_b, in_a, ssh.at[0], rsh.at[0], before, x),
        send(out_a, in_b, ssh.at[1], rsh.at[1], after, x),
    ]

    step2 = []
    for h in range(2):
        for copy in step1[h * (ny - 1):(h + 1) * (ny - 1)]:
            copy.wait_recv()
        mine = y if h == 0 else z

        def body(i, c):
            total = acc1[h, mine, i]
            for d in range(ny - 1):
                total = total + recv1[h, d, i].astype(f32)
            acc2[h, i] = total
            return c

        lax.fori_loop(0, nz, body, 0)
        for d in range(nz - 1):
            to = z_peers[d] if h == 0 else y_peers[d]
            t = place(y, to, core) if h == 0 else place(to, z, core)
            step2.append(send(acc2.at[h, to], recv2.at[h, d], ss2.at[h, d], rs2.at[h, d], t, x))

    for copy in halo:
        copy.wait_recv()
    keep = mask_ref[...].astype(f32)
    for b in range(blocks):
        total = terms_ref[FACE + b]
        if b < FACE:
            total = total + in_b[b].astype(f32)
        if b >= blocks - FACE:
            total = total + in_a[b - (blocks - FACE)].astype(f32)
        column = jnp.broadcast_to(keep[b:b + 1], total.shape).T
        grad_ref[b] = (column * total).astype(bf16)

    for h in range(2):
        for copy in step2[h * (nz - 1):(h + 1) * (nz - 1)]:
            copy.wait_recv()
        total = acc2[h, z if h == 0 else y]
        for d in range(nz - 1):
            total = total + recv2[h, d]
        share[h] = total
    recv3[x] = share[...]
    step3 = [
        send(share, recv3.at[x], ss3.at[d], rs3.at[d], tile, xx) for d, xx in enumerate(x_peers)
    ]
    for copy in step3:
        copy.wait_recv()
    total = recv3[0]
    for i in range(1, nx):
        total = total + recv3[i]
    total = total * scale
    rows = sub_ref.shape[0]
    half = total.shape[1]
    sub_ref[0:half, :] = total[0]
    sub_ref[half:rows, :] = total[1, 0:rows - half]
    down_ref[:, 0:128] = total[1, TILE_ROWS:2 * TILE_ROWS]
    down_ref[:, 128:256] = total[1, 2 * TILE_ROWS:3 * TILE_ROWS]
    for copy in copies:
        copy.wait_send()


def reduce_parts(parts, terms, mask, sizes, scale, sub_rows):
    nx, ny, nz = sizes
    rows, lanes = parts.shape[4:]
    voxels, channels = terms.shape[1:]
    f32, bf16 = jnp.float32, jnp.bfloat16
    dma = pltpu.SemaphoreType.DMA
    vmem = pl.BlockSpec(memory_space=pltpu.VMEM)
    face = (FACE, voxels, channels)
    return pl.pallas_call(
        functools.partial(reduce_kernel, sizes, scale),
        out_shape=(
            jax.ShapeDtypeStruct((sub_rows, lanes), f32),
            jax.ShapeDtypeStruct((TILE_ROWS, 2 * lanes), f32),
            jax.ShapeDtypeStruct((mask.shape[0], voxels, channels), bf16),
        ),
        in_specs=[vmem] * 3,
        out_specs=(vmem,) * 3,
        scratch_shapes=[
            pltpu.VMEM((2, ny, nz, rows, lanes), bf16),
            pltpu.VMEM((2, ny, nz, rows, lanes), bf16),
            pltpu.VMEM((2, ny, nz, rows, lanes), f32),
            pltpu.VMEM((2, ny, nz, rows, lanes), bf16),
            pltpu.VMEM((2, ny - 1, nz, rows, lanes), bf16),
            pltpu.VMEM((2, nz, rows, lanes), f32),
            pltpu.VMEM((2, nz - 1, rows, lanes), f32),
            pltpu.VMEM((nx, 2, rows, lanes), f32),
            pltpu.VMEM((2, rows, lanes), f32),
            pltpu.VMEM(face, bf16), pltpu.VMEM(face, bf16),
            pltpu.VMEM(face, bf16), pltpu.VMEM(face, bf16),
            dma((2,)), dma((2,)),
            dma((2, ny - 1)), dma((2, ny - 1)),
            dma((2, nz - 1)), dma((2, nz - 1)),
            dma((nx - 1,)), dma((nx - 1,)),
            dma((2,)), dma((2,)),
        ],
        compiler_params=pltpu.CompilerParams(
            collective_id=0, has_side_effects=True, vmem_limit_bytes=48 * 1024 * 1024
        ),
    )(parts, terms, mask)


def on_device(
    features,
    w_sub,
    w_down,
    cotangent,
    vox_mask,
    nbr_owner,
    nbr_slot,
    voxel_map,
    parent_slot,
    parent_octant,
):
    blocks = features.shape[1]
    voxels = features.shape[2]
    channels = features.shape[3]
    coarse_count = cotangent.shape[1]
    tile_index = lax.axis_index("tile")
    active = vox_mask[0] > 0
    masked = jnp.where(active[:, :, None], features[0], jnp.zeros((), jnp.bfloat16))
    halo_width = FACE
    extended = with_halo(masked, (("tile", 0),), halo_width)
    ext_count = extended.shape[0]
    owner_tile = nbr_owner[0]
    slot_index = nbr_slot[0]
    position = jnp.where(
        owner_tile == tile_index - 1,
        slot_index - (blocks - halo_width),
        jnp.where(
            owner_tile == tile_index, halo_width + slot_index, halo_width + blocks + slot_index
        ),
    )
    position = jnp.where(owner_tile >= 0, position, -1)
    sizes = (lax.axis_size("dp"), 8, lax.axis_size("tile") // 16)
    maps = jnp.transpose(voxel_map[0], (1, 0, 2)).reshape(-1, voxels)
    place = jnp.arange(16, dtype=jnp.int32)[None, :]
    octant = parent_octant[0][:, None]
    within = (
        16 * (4 * (octant // 4) + place // 4)
        + 4 * (2 * ((octant // 2) % 2) + (place // 2) % 2)
        + 2 * (octant % 2) + place % 2
    )
    target = (parent_slot[0][:, None] * cotangent.shape[2] + within).reshape(1, -1)
    coarse, grad_rows, parts = local_pass(
        position, extended, maps, w_sub, w_down.reshape(-1, w_down.shape[2]),
        cotangent[0].reshape(-1, cotangent.shape[3]), vox_mask[0], target, sizes,
    )
    coarse_out = coarse.reshape(cotangent.shape)
    grad_scale = float(lax.axis_size("dp") * lax.axis_size("tile") * blocks * voxels) ** (-0.5)
    sub_rows = w_sub.size // channels // lax.axis_size("tile")
    share_sub, share_down, grad_input = reduce_parts(
        parts, grad_rows, vox_mask[0], sizes, grad_scale, sub_rows
    )
    return (coarse_out, grad_input[None], share_sub.reshape(-1), share_down.reshape(-1))


def solution(mesh):
    in_specs = (
        P("dp", "tile", None, None),
        P(),
        P(),
        P("dp", "tile", None, None),
        P("dp", "tile", None),
        P("dp", "tile", None),
        P("dp", "tile", None),
        P("dp", "tile", None, None),
        P("dp", "tile"),
        P("dp", "tile"),
    )
    out_specs = (P("dp", "tile", None, None), P("dp", "tile", None, None), P("tile"), P("tile"))
    return jax.shard_map(
        on_device, mesh=mesh, in_specs=in_specs, out_specs=out_specs, check_vma=False
    )
```

time: 106 us -> 72.5 us (0.68)
  Pallas kernels: 77.4 us -> 50 us
  starting transfers between devices: 14.4 us -> 10.1 us
  other arithmetic: 8.41 us -> 5.42 us
    pallas_call x1, Pallas kernels: 35.6 us -> 17.5 us  [local_pass(): pl.pallas_call(functools.partial(local_kernel, sizes), out_shape=(jax.Sha...]
    pallas_call x1, Pallas kernels: 41.9 us -> 32.5 us  [reduce_parts(): pl.pallas_call(functools.partial(reduce_kernel, sizes, scale), out_shape=...]
    ppermute x2 -> x1, starting transfers between devices: 7.09 us -> 4.69 us  [with_halo(): after = lax.ppermute(first, axis, down)]
    ppermute x2 -> x1, starting transfers between devices: 7.31 us -> 5.39 us  [with_halo(): before = lax.ppermute(last, axis, up)]
    unnamed x4 -> x9, local copies, waits for them, and re-layouts: 3.09 us -> 4.94 us
    another operation x1 -> x0, other arithmetic: 1.19 us -> none
    slice x2 -> x0, local copies, waits for them, and re-layouts: 1.09 us -> none  [the longest x1 1.08 us: on_device(): own_grad = grad_rows[halo_width:halo_width + blocks]]
  transfers between devices with their start and end apart: 4 -> 2, of which waited for: 0 -> 0; matrix products, arithmetic and copies ran while one was open for 5% -> 5% of each run, Pallas kernels for 40% -> 0%
where the time goes in v1:
time: 72.5 us; the launch traced here: 71.8 us
  Pallas kernels  50 us (69%)
  starting transfers between devices  10.1 us (14%)
  local copies, waits for them, and re-layouts  5.55 us (8%)
  other arithmetic  5.42 us (7%)
    pallas_call x1, Pallas kernels, reduce_parts(): pl.pallas_call(functools.partial(reduce_kernel, sizes, scale), out_shape=...  32.5 us
    pallas_call x1, Pallas kernels, local_pass(): pl.pallas_call(functools.partial(local_kernel, sizes), out_shape=(jax.Sha...  17.5 us
    ppermute x1, starting transfers between devices, with_halo(): before = lax.ppermute(last, axis, up)  5.39 us
    unnamed x9, local copies, waits for them, and re-layouts  4.94 us
    ppermute x1, starting transfers between devices, with_halo(): after = lax.ppermute(first, axis, down)  4.69 us
  transfers between devices with their start and end apart: 2, of which 0 were waited for; matrix products, arithmetic and copies ran while one was open for 5% of the time, Pallas kernels for 0%

profile of v1, /device:TPU:1, one launch (start us, length us, event | category | flops | bytes accessed | tf_op | source)
XLA Modules:
  0.0 71.8 jit_solution(14536740333885944764)
XLA Ops:
  0.6 0.0 copy-start.2
  0.6 0.8 %broadcast_compare_fusion = pred[8,128]{1,0:T(8,128)(4,1)S(1)} fusion(s32[1,8,128]{2,1,0:T(8,128)} %param.14), kind=kLoop, calls=%fused_computation.8 | loop fusion | flops 1024 | bytes 5120 | tf_op jit(solution)/shard_map/gt | solution.py:374
  1.4 1.1 %bitcast_select_fusion = bf16[8,128,128]{2,1,0:T(8,128)(2,1)S(1)} fusion(bf16[1,8,128,128]{3,2,1,0:T(8,128)(2,1)} %param.10, pred[8,128]{1,0:T(8,128)(4,1)S(1)} %broadcast_compare_fusion), kind=kLoop, calls=%fused_computation.1 | loop fusion | flops 131072 | bytes 525312 | tf_op jit(solution)/shard_map/jit(_where)/select_n | solution.py:375
  2.6 5.4 %collective-permute-start = (bf16[2,128,128]{2,1,0:T(8,128)(2,1)S(1)}, bf16[2,128,128]{2,1,0:T(8,128)(2,1)S(1)}, u32[]{:S(2)}, u32[]{:S(2)}) collective-permute-start(bf16[2,128,128]{2,1,0:T(8,128)(2,1)S(1)} %get-tuple-element.16), channel_id=1, source_target_pairs={{0,4},{4,8},{8,12},{12,16},{16,20},{20,24},{24,28},{28,32},{32,36}... | collective-permute-start | bytes 196616 | tf_op jit(solution)/shard_map/ppermute | solution.py:21
  8.0 4.7 %collective-permute-start.1 = (bf16[2,128,128]{2,1,0:T(8,128)(2,1)S(1)}, bf16[2,128,128]{2,1,0:T(8,128)(2,1)S(1)}, u32[]{:S(2)}, u32[]{:S(2)}) collective-permute-start(bf16[2,128,128]{2,1,0:T(8,128)(2,1)S(1)} %get-tuple-element.17), channel_id=1, source_target_pairs={{4,0},{8,4},{12,8},{16,12},{20,16},{24,20},{28,24},{32,28},{36,32}... | collective-permute-start | bytes 196616 | tf_op jit(solution)/shard_map/ppermute | solution.py:22
  12.7 0.7 multiply_bitcast_fusion
  13.4 0.7 fusion.4
  14.0 1.3 %select_bitcast_fusion.pos_ref = s32[8,27]{1,0:T(8,128)} fusion(s32[1,8,27]{2,1,0:T(8,128)} %param.16, s32[1,8,27]{2,1,0:T(8,128)} %param.15, s32[]{:T(128)S(6)} %axis_index.15, s32[]{:T(128)S(6)} %sub.21), kind=kLoop, calls=%fused_computation.3 | loop fusion | flops 1944 | bytes 2600 | tf_op jit(solution)/shard_map/jit(_where)/select_n | solution.py:388
  15.3 0.1 add_add_fusion
  15.4 0.6 reshape.414.tgt_ref
  16.0 0.0 collective-permute-done
  16.0 0.0 collective-permute-done.1
  16.0 0.8 %pad_maximum_fusion.ext_ref = bf16[12,128,128]{2,1,0:T(8,128)(2,1)} fusion(bf16[2,128,128]{2,1,0:T(8,128)(2,1)S(1)} %collective-permute-done.1, bf16[8,128,128]{2,1,0:T(8,128)(2,1)S(1)} %bitcast_select_fusion, bf16[2,128,128]{2,1,0:T(8,128)(2,1)S(1)} %collective-permute-done), kind=kLoop, calls=%fused_computation | loop fusion | flops 393216 | bytes 786432 | tf_op jit(solution)/shard_map/concatenate | solution.py:23
  16.8 17.5 %shard_map.129 = (bf16[512,256]{1,0:T(8,128)(2,1)}, f32[12,128,128]{2,1,0:T(8,128)}, f32[2,2,8,8,24,128]{5,4,3,2,1,0:T(8,128)}) custom-call(s32[8,27]{1,0:T(8,128)} %select_bitcast_fusion.pos_ref, bf16[12,128,128]{2,1,0:T(8,128)(2,1)} %pad_maximum_fusion.ext_ref, s32[216,128]{1,0:T(8,128)} %bitcast.53, bf16[27,128,128]{2,1,0:T(8,128)(2,1)} %ws_ref.1, ...), custom_call_target="tpu_custom_call" | custom-call | tf_op jit(solution)/shard_map/pallas_call | solution.py:154
  34.4 0.0 copy-done.2
  34.4 0.0 copy-start
  34.4 1.9 %copy-done = f32[2,2,8,8,24,128]{5,4,3,2,1,0:T(8,128)S(1)} copy-done((f32[2,2,8,8,24,128]{5,4,3,2,1,0:T(8,128)S(1)}, f32[2,2,8,8,24,128]{5,4,3,2,1,0:T(8,128)}, u32[]{:S(2)}) %copy-start) | copy-done | bytes 3145752
  36.2 0.0 copy-start.1
  36.2 1.1 %copy-done.1 = f32[12,128,128]{2,1,0:T(8,128)S(1)} copy-done((f32[12,128,128]{2,1,0:T(8,128)S(1)}, f32[12,128,128]{2,1,0:T(8,128)}, u32[]{:S(2)}) %copy-start.1) | copy-done | bytes 786456
  37.4 32.5 %shard_map.130 = (f32[27,128]{1,0:T(8,128)S(1)}, f32[8,256]{1,0:T(8,128)S(1)}, bf16[8,128,128]{2,1,0:T(8,128)(2,1)S(1)}) custom-call(f32[2,2,8,8,24,128]{5,4,3,2,1,0:T(8,128)S(1)} %copy-done, f32[12,128,128]{2,1,0:T(8,128)S(1)} %copy-done.1, s32[8,128]{1,0:T(8,128)S(1)} %bitcast.48), custom_call_target="tpu_custom_call" | custom-call | tf_op jit(solution)/shard_map/pallas_call | solution.py:324
  69.9 0.6 copy.14
  70.5 0.7 copy.17
  71.2 0.6 copy.18
  (3 shorter events, 0.0 us)
Async XLA Ops:
  0.6 33.7 %copy-start.2 = (s32[1,8,128]{2,1,0:T(8,128)S(1)}, s32[1,8,128]{2,1,0:T(8,128)}, u32[]{:S(2)}) copy-start(s32[1,8,128]{2,1,0:T(8,128)} %param.14) | copy-start | bytes 12292
  2.6 13.4 %collective-permute-start = (bf16[2,128,128]{2,1,0:T(8,128)(2,1)S(1)}, bf16[2,128,128]{2,1,0:T(8,128)(2,1)S(1)}, u32[]{:S(2)}, u32[]{:S(2)}) collective-permute-start(bf16[2,128,128]{2,1,0:T(8,128)(2,1)S(1)} %get-tuple-element.16), channel_id=1, source_target_pairs={{0,4},{4,8},{8,12},{12,16},{16,20},{20,24},{24,28},{28,32},{32,36}... | collective-permute-start | bytes 196616 | tf_op jit(solution)/shard_map/ppermute | solution.py:21
  8.0 8.0 %collective-permute-start.1 = (bf16[2,128,128]{2,1,0:T(8,128)(2,1)S(1)}, bf16[2,128,128]{2,1,0:T(8,128)(2,1)S(1)}, u32[]{:S(2)}, u32[]{:S(2)}) collective-permute-start(bf16[2,128,128]{2,1,0:T(8,128)(2,1)S(1)} %get-tuple-element.17), channel_id=1, source_target_pairs={{4,0},{8,4},{12,8},{16,12},{20,16},{24,20},{28,24},{32,28},{36,32}... | collective-permute-start | bytes 196616 | tf_op jit(solution)/shard_map/ppermute | solution.py:22
  34.4 1.9 %copy-start = (f32[2,2,8,8,24,128]{5,4,3,2,1,0:T(8,128)S(1)}, f32[2,2,8,8,24,128]{5,4,3,2,1,0:T(8,128)}, u32[]{:S(2)}) copy-start(f32[2,2,8,8,24,128]{5,4,3,2,1,0:T(8,128)} %get-tuple-element.11.parts_ref) | copy-start | bytes 9437188
  36.2 1.1 %copy-start.1 = (f32[12,128,128]{2,1,0:T(8,128)S(1)}, f32[12,128,128]{2,1,0:T(8,128)}, u32[]{:S(2)}) copy-start(f32[12,128,128]{2,1,0:T(8,128)} %get-tuple-element.12.terms_ref) | copy-start | bytes 2359300
